TPU v7x, 512 devices: a whole 4x8x8 slice. The times are simulated.
512 devices in a mesh: blk: 16 (over x_lo, y), grp: 32 (over z, x_hi, core).
Axes of the slice: x: 4 (x_hi: 2, x_lo: 2; x = x_hi * 2 + x_lo), y: 8, z: 8, core: 2. Of those that a mesh axis runs over, the one named last changes fastest.
Arguments:
- own_tiles: bfloat16 [61440, 128, 128], P(('blk', 'grp')), may hold values from 4 to 24865, as said below
- own_rows: int32 [61440], P(('blk', 'grp')), may hold values from 0 to 31
- own_cols: int32 [61440], P(('blk', 'grp')), may hold values from 0 to 15
- hub_tiles: bfloat16 [8192, 1, 128, 128], P(('blk', 'grp')), may hold values from 4 to 24865, as said below
- hub_rows: int32 [8192, 1], P(('blk', 'grp')), may hold values from 0 to 31
- hub_cols: int32 [8192, 1], P(('blk', 'grp')), may hold values from 0 to 15
- factor: float32 [65536, 128], P(('blk', 'grp')), may hold values from 0.001 to 25, as said below
Outputs:
- updated: float32 [65536, 128], P(('blk', 'grp'))
Inputs may be any that keep to these rules, and one draw needn't show every extreme that they name: `hub_rows`: every device holds exactly 120 own tiles and 1 hub tiles for each index of blk; tiles may share coordinates, and then they add. `factor`: every entry is positive. `own_tiles`: every entry is positive. `hub_tiles`: every entry is positive.
All inputs are finite; a program needn't handle non-finite values.
Results may differ from a plain program's by a relative error of at most 0.0015.
Values may be sent and summed in bfloat16 or wider, within the bound.
A program may use at most 64 MiB of HBM per device.

v0:
```python
import jax
import jax.numpy as jnp
from jax import lax
from jax.sharding import PartitionSpec as P

ITERS = 2


damping = 0.5


def body(own_tiles, own_rows, own_cols, hub_tiles, hub_rows, hub_cols, factor):
    tile_size = own_tiles.shape[1]
    factor_width = factor.shape[1]
    rows_local = factor.shape[0]
    row_count = lax.axis_size("grp") * rows_local // tile_size
    current = factor
    for sweep in range(ITERS):
        low_factor = current.astype(jnp.bfloat16)
        gathered = lax.all_gather(low_factor, "blk", axis=0, tiled=True)
        col_blocks = gathered.reshape(-1, tile_size, factor_width)
        gram_matrix = lax.psum(
            jnp.dot(low_factor.T, low_factor, preferred_element_type=jnp.float32), ("blk", "grp")
        )
        own_products = jnp.einsum(
            "tij,tjk->tik", own_tiles, col_blocks[own_cols], preferred_element_type=jnp.float32
        )
        helper_made = jnp.einsum(
            "dhij,dhjk->dhik", hub_tiles, col_blocks[hub_cols], preferred_element_type=jnp.float32
        )
        hub_products, dest_rows = (
            lax.all_to_all(
                helper_made.astype(jnp.bfloat16), "blk", split_axis=0, concat_axis=0, tiled=True
            ).astype(helper_made.dtype),
            lax.all_to_all(hub_rows, "blk", split_axis=0, concat_axis=0, tiled=True),
        )
        products = jnp.concatenate(
            [own_products, hub_products.reshape(-1, tile_size, factor_width)], axis=0
        )
        all_rows = jnp.concatenate([own_rows, dest_rows.reshape(-1)], axis=0)
        partials = jax.ops.segment_sum(products, all_rows, num_segments=row_count).reshape(
            -1, factor_width
        )
        product_rows = lax.psum_scatter(partials, "grp", scatter_dimension=0, tiled=True)
        curvature = jnp.dot(current, gram_matrix, precision=lax.Precision.HIGHEST)
        current = current * (1.0 - damping + damping * product_rows / curvature)
    return current


def solution(mesh):
    in_specs = (
        P(("blk", "grp"), None, None),
        P(("blk", "grp")),
        P(("blk", "grp")),
        P(("blk", "grp"), None, None, None),
        P(("blk", "grp"), None),
        P(("blk", "grp"), None),
        P(("blk", "grp"), None),
    )
    out_specs = P(("blk", "grp"), None)
    return jax.shard_map(body, mesh=mesh, in_specs=in_specs, out_specs=out_specs, check_vma=False)
```

profile of v0, /device:TPU:1, one launch (start us, length us, event | category | flops | bytes accessed | tf_op | source)
XLA Modules:
  0.0 605.2 jit_solution(5017200888271714587)
XLA Ops:
  7.4 1.4 copy.42
  8.8 8.7 %all-to-all-start = ((s32[16,1,1]{2,1,0:T(1,128)}), s32[16,1,1]{2,1,0:T(1,128)S(1)}, u32[]{:S(2)}, u32[]{:S(2)}) async-start(s32[16,1,1]{2,1,0:T(1,128)} %copy.42), calls=%async_computation | async-start | bytes 16384 | tf_op jit(solution)/shard_map/all_to_all | solution.py:35
  19.2 28.8 %all_gather.6 = bf16[2048,128]{1,0:T(8,128)(2,1)S(1)} all-gather(bf16[128,128]{1,0:T(8,128)(2,1)S(1)} %convert_element_type.26), channel_id=1, replica_groups=mesh['blk'=16,'grp'=32] {'blk'}, dimensions={0}, use_global_device_ids=true | all-gather | bytes 557056 | tf_op jit(solution)/shard_map/all_gather | solution.py:20
  49.3 1.3 fusion
  50.7 3.6 all-to-all-start.1
  54.3 2.9 gather_fusion
  57.3 9.3 %convolution_bitcast_fusion.1 = f32[120,128,128]{1,2,0:T(8,128)} fusion(bf16[120,128,128]{2,1,0:T(8,128)(2,1)} %gather_fusion, bf16[120,128,128]{2,1,0:T(8,128)(2,1)} %param.7), kind=kOutput, calls=%fused_computation.9 | convolution fusion | flops 503316480 | bytes 15728640 | tf_op jit(solution)/shard_map/tij,tjk->tik/dot_general | solution.py:25
  67.1 8.0 %pad_maximum_fusion = f32[136,128,128]{1,2,0:T(8,128)} fusion(f32[16,128,128]{1,2,0:T(8,128)S(1)} %bitcast_convert_fusion.1, f32[120,128,128]{1,2,0:T(8,128)} %convolution_bitcast_fusion.1), kind=kLoop, calls=%fused_computation.6 | loop fusion | flops 2228224 | bytes 17825792 | tf_op jit(solution)/shard_map/concatenate | solution.py:37
  75.1 9.3 %copy.47 = f32[136,128,128]{2,1,0:T(8,128)} copy(f32[136,128,128]{1,2,0:T(8,128)} %pad_maximum_fusion) | data formatting | bytes 17825792 | tf_op jit(solution)/shard_map/concatenate | solution.py:37
  84.7 19.0 %scatter_fusion = f32[32,128,128]{2,1,0:T(8,128)S(1)} fusion(f32[32,128,128]{2,1,0:T(8,128)S(1)} %broadcast.18.clone, s32[136]{0:T(256)S(1)} %pad_add_fusion, f32[136,128,128]{2,1,0:T(8,128)} %copy.47), kind=kCustom, calls=%fused_computation.4 | custom fusion | flops 2228224 | bytes 26739232 | tf_op jit(solution)/shard_map/scatter-add | solution.py:41
  103.7 1.8 copy.65
  105.6 186.9 %all-reduce.3.cloned.1.call-done = f32[128,128]{1,0:T(8,128)} async-done(((f32[128,128]{1,0:T(8,128)}), f32[128,128]{1,0:T(8,128)}) %all-reduce.3.cloned.1.call-update) | async-done | bytes 65552 | tf_op jit(solution)/shard_map/psum | solution.py:22
  292.5 1.2 fusion.10
  293.7 26.6 %all_gather.7 = bf16[2048,128]{0,1:T(8,128)(2,1)S(1)} all-gather(bf16[128,128]{0,1:T(8,128)(2,1)S(1)} %get-tuple-element.5), channel_id=1, replica_groups=mesh['blk'=16,'grp'=32] {'blk'}, dimensions={0}, use_global_device_ids=true | all-gather | bytes 557056 | tf_op jit(solution)/shard_map/all_gather | solution.py:20
  321.2 1.3 fusion.1
  322.5 3.6 all-to-all-start.2
  326.1 2.9 gather_fusion.2
  330.1 9.3 %convolution_bitcast_fusion = f32[120,128,128]{1,2,0:T(8,128)} fusion(bf16[120,128,128]{2,1,0:T(8,128)(2,1)} %gather_fusion.2, bf16[120,128,128]{2,1,0:T(8,128)(2,1)} %param.7), kind=kOutput, calls=%fused_computation.8 | convolution fusion | flops 503316480 | bytes 15728640 | tf_op jit(solution)/shard_map/tij,tjk->tik/dot_general | solution.py:25
  339.5 8.0 %pad_maximum_fusion.1 = f32[136,128,128]{1,2,0:T(8,128)} fusion(f32[16,128,128]{1,2,0:T(8,128)S(1)} %bitcast_convert_fusion, f32[120,128,128]{1,2,0:T(8,128)} %convolution_bitcast_fusion), kind=kLoop, calls=%fused_computation.7 | loop fusion | flops 2228224 | bytes 17825792 | tf_op jit(solution)/shard_map/concatenate | solution.py:37
  347.5 9.3 %copy.56 = f32[136,128,128]{2,1,0:T(8,128)} copy(f32[136,128,128]{1,2,0:T(8,128)} %pad_maximum_fusion.1) | data formatting | bytes 17825792 | tf_op jit(solution)/shard_map/concatenate | solution.py:37
  357.1 18.9 %scatter_fusion.1 = f32[32,128,128]{2,1,0:T(8,128)S(1)} fusion(f32[32,128,128]{2,1,0:T(8,128)S(1)} %broadcast.18, s32[136]{0:T(256)S(1)} %pad_add_fusion, f32[136,128,128]{2,1,0:T(8,128)} %copy.56), kind=kCustom, calls=%fused_computation.5 | custom fusion | flops 2228224 | bytes 26739232 | tf_op jit(solution)/shard_map/scatter-add | solution.py:41
  376.0 1.8 copy.66
  377.9 218.0 %all-reduce.5.cloned.1.call-done = f32[128,128]{1,0:T(8,128)} async-done(((f32[128,128]{1,0:T(8,128)}), f32[128,128]{1,0:T(8,128)}) %all-reduce.5.cloned.1.call-update) | async-done | bytes 65552 | tf_op jit(solution)/shard_map/psum | solution.py:22
  595.8 1.2 fusion.3
  (41 shorter events, 7.1 us)
Async XLA Ops:
  7.4 42.0 %copy-start = (bf16[16,1,128,128]{3,2,1,0:T(8,128)(2,1)S(1)}, bf16[16,1,128,128]{3,2,1,0:T(8,128)(2,1)}, u32[]{:S(2)}) copy-start(bf16[16,1,128,128]{3,2,1,0:T(8,128)(2,1)} %param.10) | copy-start | bytes 1572868
  7.4 46.9 %copy-start.4 = (s32[120]{0:T(128)S(1)}, s32[120]{0:T(128)}, u32[]{:S(2)}) copy-start(s32[120]{0:T(128)} %param.9) | copy-start | bytes 1444
  8.8 41.9 %all-to-all-start = ((s32[16,1,1]{2,1,0:T(1,128)}), s32[16,1,1]{2,1,0:T(1,128)S(1)}, u32[]{:S(2)}, u32[]{:S(2)}) async-start(s32[16,1,1]{2,1,0:T(1,128)} %copy.42), calls=%async_computation | async-start | bytes 16384 | tf_op jit(solution)/shard_map/all_to_all | solution.py:35
  17.4 275.1 %all-reduce.3.cloned.1.call-start = ((), (), s32[]{:S(2)}) async-start(), calls=%async_computation.6 | async-start | bytes 131072 | tf_op jit(solution)/shard_map/psum | solution.py:22
  50.7 16.3 %all-to-all-start.1 = ((bf16[16,1,128,128]{2,3,1,0:T(8,128)(2,1)}), bf16[16,1,128,128]{2,3,1,0:T(8,128)(2,1)S(1)}, u32[]{:S(2)}, u32[]{:S(2)}) async-start(bf16[16,1,128,128]{2,3,1,0:T(8,128)(2,1)} %fusion), calls=%async_computation.1 | async-start | bytes 1048576 | tf_op jit(solution)/shard_map/all_to_all | solution.py:32
  54.2 238.3 %reduce-scatter.3.cloned.1.call-start = ((), (), s32[]{:S(2)}) async-start(), calls=%async_computation.5 | async-start | bytes 2162688 | tf_op jit(solution)/shard_map/reduce_scatter | solution.py:44
  57.3 9.7 %copy-start.3 = (s32[120]{0:T(128)S(1)}, s32[120]{0:T(128)}, u32[]{:S(2)}) copy-start(s32[120]{0:T(128)} %param.8) | copy-start | bytes 1444
  103.6 1.9 copy-start.2
  322.5 16.9 %all-to-all-start.2 = ((bf16[16,1,128,128]{2,3,1,0:T(8,128)(2,1)}), bf16[16,1,128,128]{2,3,1,0:T(8,128)(2,1)S(1)}, u32[]{:S(2)}, u32[]{:S(2)}) async-start(bf16[16,1,128,128]{2,3,1,0:T(8,128)(2,1)} %fusion.1), calls=%async_computation.3 | async-start | bytes 1048576 | tf_op jit(solution)/shard_map/all_to_all | solution.py:32
  326.1 269.7 %all-reduce.5.cloned.1.call-start = ((), (), s32[]{:S(2)}) async-start(), calls=%async_computation.8 | async-start | bytes 131072 | tf_op jit(solution)/shard_map/psum | solution.py:22
  329.9 266.0 %reduce-scatter.5.cloned.1.call-start = ((), (), s32[]{:S(2)}) async-start(), calls=%async_computation.7 | async-start | bytes 2162688 | tf_op jit(solution)/shard_map/reduce_scatter | solution.py:44
  357.1 240.7 %copy-start.1 = (bf16[16,1,128,128]{3,2,1,0:T(8,128)(2,1)S(1)}, bf16[16,1,128,128]{3,2,1,0:T(8,128)(2,1)}, u32[]{:S(2)}) copy-start(bf16[16,1,128,128]{3,2,1,0:T(8,128)(2,1)} %param.10) | copy-start | bytes 1572868
Sparse Core Ops, SparseCore 0:
  23.3 269.1 all-reduce.2
  331.9 263.8 all-reduce.4
Sparse Core Ops, SparseCore 1:
  105.6 135.3 reduce-scatter.2
  378.0 126.7 reduce-scatter.4
where the time goes:
time: 607 us; the launch traced here: 605 us
  waiting for transfers between devices  405 us (67%)
  other arithmetic  56.1 us (9%)
  blocking collectives  55.4 us (9%)
  local copies, waits for them, and re-layouts  32.4 us (5%)
  matrix products  25.1 us (4%)
  starting transfers between devices  16.2 us (3%)
  between operations  15.1 us (2%)
    psum x2, waiting for transfers between devices, body(): lax.psum(jnp.dot(low_factor.T, low_factor, preferred_element_type=jnp.flo...  405 us
    all_gather x2, blocking collectives, body(): gathered = lax.all_gather(low_factor, 'blk', axis=0, tiled=True)  55.4 us
    scatter-add x2, other arithmetic, body(): jax.ops.segment_sum(products, all_rows, num_segments=row_count)  37.9 us
    concatenate x2, local copies, waits for them, and re-layouts, body(): jnp.concatenate([own_products, hub_products.reshape(-1, tile_size, factor...  18.6 us
    dot_general x2, matrix products, body(): jnp.einsum('tij,tjk->tik', own_tiles, col_blocks[own_cols], preferred_ele...  18.5 us
    concatenate x2, other arithmetic, body(): jnp.concatenate([own_products, hub_products.reshape(-1, tile_size, factor...  16 us
  transfers between devices with their start and end apart: 7, of which 2 were waited for; matrix products, arithmetic and copies ran while one was open for 18% of the time, Pallas kernels for 0%

commit v1 on v0

v1 whole, which is shorter than its diff:
```python
import jax
import jax.numpy as jnp
from jax import lax
from jax.experimental import pallas as pl
from jax.experimental.pallas import tpu as pltpu
from jax.sharding import PartitionSpec as P

ITERS = 2
T = 128
NB = 16
NG = 32
NZ = 8
OWN = 120
MESH = pl.DeviceIdType.MESH
damping = 0.5

RING = (4, 3, 5, 2, 6, 1, 7)
BLK_ORDER = tuple((h, k) for k in (4, 3, 5, 2, 6, 1, 7) for h in (1, 0)) + ((1, 0),)


def kernel(own_hbm, own_rows, own_cols, hub_hbm, hub_rows, hub_cols, factor, out,
           own_v, hub_v, meta, meta_in, gath0, gath1, acc, ptr_v, ptr_s,
           send_a, send_b, send_c, recv_a0, recv_a1, recv_b0, recv_b1, recv_c0, recv_c1,
           gram_own, gram_in0, gram_in1, gram0, gram1,
           local_sem, ptr_sem, meta_ssem, meta_rsem, hub_ssem, hub_rsem,
           ag_ssem, ag_rsem, a_ssem, a_rsem, b_ssem, b_rsem, c_ssem, c_rsem,
           g_ssem, g_rsem, h_ssem, h_rsem):
    b, g = lax.axis_index("blk"), lax.axis_index("grp")
    y = lax.rem(b, NZ)
    half = b // NZ
    c = lax.rem(g, 2)
    xh = lax.rem(g, 4) // 2
    z = g // 4

    def blk_peer(h, k):
        return lax.rem(half + h, 2) * NZ + lax.rem(y + k, NZ)

    def wait(like, sem):
        pltpu.make_async_copy(like, like, sem).wait()

    tiles_copy = pltpu.make_async_copy(own_hbm, own_v, local_sem.at[0])
    tiles_copy.start()
    hub_copy = pltpu.make_async_copy(hub_hbm.at[b], hub_v.at[b], local_sem.at[1])
    hub_copy.start()

    barrier = pltpu.get_barrier_semaphore()
    for h, k in BLK_ORDER:
        pl.semaphore_signal(barrier, inc=1, device_id=(blk_peer(h, k), g), device_id_type=MESH)

    def greet(k, _):
        pl.semaphore_signal(barrier, inc=1, device_id=(b, lax.rem(g + k, NG)), device_id_type=MESH)
        return 0

    lax.fori_loop(1, NG, greet, 0)

    for d in range(NB):
        meta[d] = jnp.full((8, T), hub_rows[d, 0] * NB + hub_cols[d, 0], jnp.int32)
    acc[0] = jnp.zeros((T, T), jnp.float32)
    low = factor[...].astype(jnp.bfloat16)
    gath0[b] = low

    pl.semaphore_wait(barrier, NB - 1 + NG - 1)

    def send_factor(gath, sweep):
        for h, k in BLK_ORDER:
            pltpu.make_async_remote_copy(
                gath.at[b], gath.at[b], ag_ssem.at[sweep], ag_rsem.at[sweep],
                device_id=(blk_peer(h, k), g), device_id_type=MESH).start()

    for h, k in BLK_ORDER:
        d = blk_peer(h, k)
        pltpu.make_async_remote_copy(
            meta.at[d], meta_in.at[b], meta_ssem, meta_rsem, device_id=(d, g), device_id_type=MESH).start()
    send_factor(gath0, 0)
    for h, k in BLK_ORDER:
        d = blk_peer(h, k)
        pltpu.make_async_remote_copy(
            hub_hbm.at[d], hub_v.at[b], hub_ssem, hub_rsem, device_id=(d, g), device_id_type=MESH).start()
    meta_in[b] = meta[b]

    lane = lax.broadcasted_iota(jnp.int32, (8, T), 1)
    sub = lax.broadcasted_iota(jnp.int32, (8, T), 0)

    def lay(u, rows):
        return jnp.where(lane == u, own_rows[u], rows)

    rows = lax.fori_loop(0, OWN, lay, jnp.full((8, T), -1, jnp.int32), unroll=8)
    wait(meta_in.at[pl.ds(0, NB - 1)], meta_rsem)
    hub_r = jnp.full((8, T), -1, jnp.int32)
    hub_c = jnp.zeros((8, T), jnp.int32)
    for e in range(NB):
        v = meta_in[e]
        hub_r = jnp.where(lane == e, v // NB, hub_r)
        hub_c = jnp.where(lane == e, lax.rem(v, NB), hub_c)

    def chain(u, state):
        prev_o, prev_h, last = state
        r = own_rows[u]
        prev_o = jnp.where((rows == r) & (lane > u), u + 1, prev_o)
        prev_h = jnp.where(hub_r == r, u + 1, prev_h)
        last = jnp.where(lane == r, u + 1, last)
        return prev_o, prev_h, last

    zeros = jnp.zeros((8, T), jnp.int32)
    prev_o, prev_h, last = lax.fori_loop(0, OWN, chain, (zeros, zeros, zeros), unroll=8)
    for e in range(NB):
        r = meta_in[e] // NB
        prev_h = jnp.where((hub_r == r) & (lane > e), OWN + e + 1, prev_h)
        last = jnp.where(lane == r, OWN + e + 1, last)
    ptr_v[...] = jnp.where(sub == 0, prev_o, jnp.where(sub == 1, prev_h, jnp.where(sub == 2, last, hub_c)))
    ptr_copy = pltpu.make_async_copy(ptr_v, ptr_s, ptr_sem)
    ptr_copy.start()
    ptr_copy.wait()

    def row_sum(zz, hh, cc):
        return acc[ptr_s[2, zz * 4 + hh * 2 + cc]]

    current = factor[...]
    for sweep in range(ITERS):
        gath, recv_a, recv_b, recv_c, gram_in, gram = (
            (gath0, recv_a0, recv_b0, recv_c0, gram_in0, gram0),
            (gath1, recv_a1, recv_b1, recv_c1, gram_in1, gram1),
        )[sweep]
        if sweep:
            gath[b] = current.astype(jnp.bfloat16)
            send_factor(gath, sweep)
        wait(gath.at[pl.ds(0, NB - 1)], ag_rsem.at[sweep])

        every = gath[...].reshape(NB * T, T)
        group = lax.dot_general(every, every, (((0,), (0,)), ((), ())), preferred_element_type=jnp.float32)
        if sweep:
            wait(gram_in0.at[pl.ds(0, NG - 1)], g_ssem.at[0])
        gram_own[...] = group.reshape(NB, 8, T)

        def send_gram(k, _):
            pltpu.make_async_remote_copy(
                gram_own.at[b], gram_in.at[g], g_ssem.at[sweep], g_rsem.at[sweep],
                device_id=(b, lax.rem(g + k, NG)), device_id_type=MESH).start()
            return 0

        lax.fori_loop(1, NG, send_gram, 0)
        gram_in[g] = gram_own[b]

        if sweep == 0:
            tiles_copy.wait()

        def own_step(t, _):
            p = jnp.dot(own_v[t], gath[own_cols[t]], preferred_element_type=jnp.float32)
            acc[t + 1] = acc[ptr_s[0, t]] + p
            return 0

        lax.fori_loop(0, OWN, own_step, 0, unroll=8)

        wait(gram_in.at[pl.ds(0, NG - 1)], g_rsem.at[sweep])
        gram[b] = jnp.sum(gram_in[...], axis=0)
        for h, k in BLK_ORDER:
            pltpu.make_async_remote_copy(
                gram.at[b], gram.at[b], h_ssem.at[sweep], h_rsem.at[sweep],
                device_id=(blk_peer(h, k), g), device_id_type=MESH).start()

        if sweep == 0:
            hub_copy.wait()
            wait(hub_v.at[pl.ds(0, NB - 1)], hub_rsem)

        def hub_step(t, _):
            p = jnp.dot(hub_v[t], gath[ptr_s[3, t]], preferred_element_type=jnp.float32)
            acc[OWN + t + 1] = acc[ptr_s[1, t]] + p
            return 0

        lax.fori_loop(0, NB, hub_step, 0, unroll=8)

        if sweep:
            wait(send_a, a_ssem)
            wait(send_b, b_ssem)
            wait(send_c.at[pl.ds(0, NZ - 1)], c_ssem)
        for j in range(2):
            hh = lax.rem(xh + 1 + j, 2)

            def lay_a(k, _):
                send_a[j * NZ + k] = row_sum(k, hh, 1 - c).astype(jnp.bfloat16)
                return 0

            lax.fori_loop(0, NZ, lay_a, 0, unroll=4)
            part = pl.ds(j * NZ, NZ)
            pltpu.make_async_remote_copy(
                send_a.at[part], recv_a.at[part], a_ssem, a_rsem.at[sweep, j],
                device_id=(b, g + 1 - 2 * c), device_id_type=MESH).start()
        wait(recv_a.at[pl.ds(0, NZ)], a_rsem.at[sweep, 0])
        for k in RING + (0,):
            zz = lax.rem(z + k, NZ)
            send_b[zz] = (row_sum(zz, 1 - xh, c) + recv_a[zz].astype(jnp.float32)).astype(jnp.bfloat16)
            pltpu.make_async_remote_copy(
                send_b.at[zz], recv_b.at[zz], b_ssem, b_rsem.at[sweep, zz],
                device_id=(b, g + 2 - 4 * xh), device_id_type=MESH).start()
        wait(recv_a.at[pl.ds(NZ, NZ)], a_rsem.at[sweep, 1])
        total = None
        for k in RING + (0,):
            zz = lax.rem(z + k, NZ)
            mine = row_sum(zz, xh, c) + recv_a[NZ + zz].astype(jnp.float32)
            wait(recv_b.at[zz], b_rsem.at[sweep, zz])
            total = mine + recv_b[zz].astype(jnp.float32)
            if k:
                send_c[zz] = total.astype(jnp.bfloat16)
                pltpu.make_async_remote_copy(
                    send_c.at[zz], recv_c.at[z], c_ssem, c_rsem.at[sweep],
                    device_id=(b, zz * 4 + xh * 2 + c), device_id_type=MESH).start()

        wait(gram.at[pl.ds(0, NB - 1)], h_rsem.at[sweep])
        curvature = jnp.dot(current, gram[...].reshape(T, T), precision=lax.Precision.HIGHEST,
                            preferred_element_type=jnp.float32)
        wait(recv_c.at[pl.ds(0, NZ - 1)], c_rsem.at[sweep])
        for k in RING:
            total = total + recv_c[lax.rem(z + k, NZ)].astype(jnp.float32)
        current = current * (1.0 - damping + damping * total / curvature)

    out[...] = current
    wait(meta_in.at[pl.ds(0, NB - 1)], meta_ssem)
    wait(hub_v.at[pl.ds(0, NB - 1)], hub_ssem)
    wait(gram_in1.at[pl.ds(0, NG - 1)], g_ssem.at[1])
    for sweep in range(ITERS):
        wait(gath0.at[pl.ds(0, NB - 1)], ag_ssem.at[sweep])
        wait(gram0.at[pl.ds(0, NB - 1)], h_ssem.at[sweep])
    wait(send_a, a_ssem)
    wait(send_b, b_ssem)
    wait(send_c.at[pl.ds(0, NZ - 1)], c_ssem)


def body(own_tiles, own_rows, own_cols, hub_tiles, hub_rows, hub_cols, factor):
    bf, f32, i32 = jnp.bfloat16, jnp.float32, jnp.int32
    V, S, D = pltpu.VMEM, pltpu.SMEM, pltpu.SemaphoreType.DMA
    vmem, smem, hbm = (pl.BlockSpec(memory_space=m) for m in (V, S, pl.ANY))
    return pl.pallas_call(
        kernel,
        out_shape=jax.ShapeDtypeStruct((T, T), f32),
        in_specs=[hbm, smem, smem, hbm, smem, smem, vmem],
        out_specs=vmem,
        scratch_shapes=[
            V((OWN, T, T), bf), V((NB, T, T), bf), V((NB, 8, T), i32), V((NB, 8, T), i32),
            V((NB, T, T), bf), V((NB, T, T), bf), V((OWN + NB + 1, T, T), f32), V((8, T), i32), S((8, T), i32),
            V((2 * NZ, T, T), bf), V((NZ, T, T), bf), V((NZ, T, T), bf),
            V((2 * NZ, T, T), bf), V((2 * NZ, T, T), bf), V((NZ, T, T), bf), V((NZ, T, T), bf),
            V((NZ, T, T), bf), V((NZ, T, T), bf),
            V((NB, 8, T), f32), V((NG, 8, T), f32), V((NG, 8, T), f32), V((NB, 8, T), f32), V((NB, 8, T), f32),
            D((2,)), D, D, D, D, D,
            D((2,)), D((2,)), D, D((2, 2)), D, D((2, NZ)), D, D((2,)),
            D((2,)), D((2,)), D((2,)), D((2,)),
        ],
        compiler_params=pltpu.CompilerParams(
            collective_id=1, has_side_effects=True, vmem_limit_bytes=48 << 20),
    )(own_tiles, own_rows, own_cols, hub_tiles.reshape(NB, T, T), hub_rows, hub_cols, factor)


def solution(mesh):
    in_specs = (
        P(("blk", "grp"), None, None),
        P(("blk", "grp")),
        P(("blk", "grp")),
        P(("blk", "grp"), None, None, None),
        P(("blk", "grp"), None),
        P(("blk", "grp"), None),
        P(("blk", "grp"), None),
    )
    out_specs = P(("blk", "grp"), None)
    return jax.shard_map(body, mesh=mesh, in_specs=in_specs, out_specs=out_specs, check_vma=False)
```

time: 607 us -> 101 us (0.17)
  waiting for transfers between devices: 405 us -> 0 us
  Pallas kernels: 0 us -> 93 us
  other arithmetic: 56.1 us -> 0 us
  blocking collectives: 55.4 us -> 0 us
  matrix products: 25.1 us -> 0 us
  local copies, waits for them, and re-layouts: 32.4 us -> 7.4 us
  starting transfers between devices: 16.2 us -> 0 us
  between operations: 15.1 us -> 0.02 us
    psum x2 -> x0, waiting for transfers between devices: 405 us -> none  [body(): lax.psum(jnp.dot(low_factor.T, low_factor, preferred_element_type=jnp.flo...]
    pallas_call x0 -> x1, Pallas kernels: none -> 93 us  [body(): pl.pallas_call(kernel, out_shape=jax.ShapeDtypeStruct((T, T), f32), in_sp...]
    all_gather x2 -> x0, blocking collectives: 55.4 us -> none  [body(): gathered = lax.all_gather(low_factor, 'blk', axis=0, tiled=True)]
    scatter-add x2 -> x0, other arithmetic: 37.9 us -> none  [body(): jax.ops.segment_sum(products, all_rows, num_segments=row_count)]
    dot_general x8 -> x0, matrix products: 25.1 us -> none  [the longest x2 18.5 us: body(): jnp.einsum('tij,tjk->tik', own_tiles, col_blocks[own_cols], preferred_ele...]
    concatenate x2 -> x0, local copies, waits for them, and re-layouts: 18.6 us -> none  [body(): jnp.concatenate([own_products, hub_products.reshape(-1, tile_size, factor...]
    concatenate x3 -> x0, other arithmetic: 16.1 us -> none  [the longest x2 16 us: body(): jnp.concatenate([own_products, hub_products.reshape(-1, tile_size, factor...]
    all_to_all x3 -> x0, starting transfers between devices: 15.8 us -> none  [the longest x1 8.68 us: body(): lax.all_to_all(hub_rows, 'blk', split_axis=0, concat_axis=0, tiled=True)]
  transfers between devices with their start and end apart: 7 -> 0, of which waited for: 2 -> 0; matrix products, arithmetic and copies ran while one was open for 18% -> 0% of each run, Pallas kernels for 0% -> 0%
where the time goes in v1:
time: 101 us; the launch traced here: 100 us
  Pallas kernels  93 us (92%)
  local copies, waits for them, and re-layouts  7.4 us (7%)
    pallas_call x1, Pallas kernels, body(): pl.pallas_call(kernel, out_shape=jax.ShapeDtypeStruct((T, T), f32), in_sp...  93 us
    unnamed x13, local copies, waits for them, and re-layouts  7.4 us

profile of v1, /device:TPU:1, one launch (start us, length us, event | category | flops | bytes accessed | tf_op | source)
XLA Modules:
  0.0 100.4 jit_solution(7087095996243188866)
XLA Ops:
  0.0 0.7 copy.8.hub_rows
  0.7 0.7 copy.9.hub_cols
  1.5 0.0 copy-start
  1.5 2.1 %copy-done = bf16[120,128,128]{2,1,0:T(8,128)(2,1)S(1)} copy-done((bf16[120,128,128]{2,1,0:T(8,128)(2,1)S(1)}, bf16[120,128,128]{2,1,0:T(8,128)(2,1)}, u32[]{:S(2)}) %copy-start) | copy-done | bytes 3932184
  3.6 0.0 copy-start.1
  3.6 1.0 %copy-done.1 = bf16[16,1,128,128]{3,2,1,0:T(8,128)(2,1)S(1)} copy-done((bf16[16,1,128,128]{3,2,1,0:T(8,128)(2,1)S(1)}, bf16[16,1,128,128]{3,2,1,0:T(8,128)(2,1)}, u32[]{:S(2)}) %copy-start.1) | copy-done | bytes 524312
  4.6 0.0 copy-start.2
  4.6 0.8 copy-done.2
  5.5 0.0 copy-start.3
  5.5 0.7 copy-done.3
  6.1 0.0 copy-start.4
  6.1 0.7 copy-done.4
  6.8 93.0 %shard_map.73 = f32[128,128]{1,0:T(8,128)S(1)} custom-call(bf16[120,128,128]{2,1,0:T(8,128)(2,1)S(1)} %copy-done, s32[120]{0:T(128)S(1)} %copy-done.3, s32[120]{0:T(128)S(1)} %copy-done.4, bf16[16,128,128]{2,1,0:T(8,128)(2,1)S(1)} %bitcast.1, s32[16,1]{1,0:T(8,128)S(1)} %copy.8.hub_rows, s32[16,1]{1,0:T(8,128)S(1)} %copy.9.hub_cols, f32[128,128]{1,0:T(8,128)S(1)} %copy-done.2), custom_call_target="tpu_custom_call" | custom-call | tf_op jit(solution)/shard_map/pallas_call | solution.py:232
  99.7 0.6 copy.11
Async XLA Ops:
  1.5 2.1 %copy-start = (bf16[120,128,128]{2,1,0:T(8,128)(2,1)S(1)}, bf16[120,128,128]{2,1,0:T(8,128)(2,1)}, u32[]{:S(2)}) copy-start(bf16[120,128,128]{2,1,0:T(8,128)(2,1)} %own_hbm.1) | copy-start | bytes 11796484
  3.6 1.0 %copy-start.1 = (bf16[16,1,128,128]{3,2,1,0:T(8,128)(2,1)S(1)}, bf16[16,1,128,128]{3,2,1,0:T(8,128)(2,1)}, u32[]{:S(2)}) copy-start(bf16[16,1,128,128]{3,2,1,0:T(8,128)(2,1)} %param.10) | copy-start | bytes 1572868
  4.6 0.8 copy-start.2
  5.5 0.7 copy-start.3
  6.1 0.7 copy-start.4

commit v2 on v1

--- a/solution.py
+++ b/solution.py
@@ -18,13 +18,13 @@
 BLK_ORDER = tuple((h, k) for k in (4, 3, 5, 2, 6, 1, 7) for h in (1, 0)) + ((1, 0),)
 
 
-def kernel(own_hbm, own_rows, own_cols, hub_hbm, hub_rows, hub_cols, factor, out,
-           own_v, hub_v, meta, meta_in, gath0, gath1, acc, ptr_v, ptr_s,
+def kernel(own_hbm, own_rows_hbm, own_cols_hbm, hub_hbm, hub_rows_hbm, hub_cols_hbm, factor_hbm, out,
+           own_rows, own_cols, hub_rows, hub_cols, factor, own_v, hub_v, meta, meta_in, gath0, gath1, acc, ptr_v, ptr_s,
            send_a, send_b, send_c, recv_a0, recv_a1, recv_b0, recv_b1, recv_c0, recv_c1,
-           gram_own, gram_in0, gram_in1, gram0, gram1,
+           gram_own0, gram_own1, blk_in0, blk_in1, quad_in0, quad_in1, z_in0, z_in1, gram0, gram1,
            local_sem, ptr_sem, meta_ssem, meta_rsem, hub_ssem, hub_rsem,
            ag_ssem, ag_rsem, a_ssem, a_rsem, b_ssem, b_rsem, c_ssem, c_rsem,
-           g_ssem, g_rsem, h_ssem, h_rsem):
+           gb_ssem, gb_rsem, gq_ssem, gq_rsem, gz_ssem, gz_rsem, h_ssem, h_rsem):
     b, g = lax.axis_index("blk"), lax.axis_index("grp")
     y = lax.rem(b, NZ)
     half = b // NZ
@@ -35,9 +35,23 @@
     def blk_peer(h, k):
         return lax.rem(half + h, 2) * NZ + lax.rem(y + k, NZ)
 
+    def quad(k):
+        return g // 4 * 4 + lax.rem(g + k, 4)
+
+    def z_peer(k):
+        return lax.rem(g + 4 * k, NG)
+
     def wait(like, sem):
         pltpu.make_async_copy(like, like, sem).wait()
 
+    small = [
+        pltpu.make_async_copy(src, dst, local_sem.at[2 + i])
+        for i, (src, dst) in enumerate((
+            (factor_hbm, factor), (hub_rows_hbm, hub_rows), (hub_cols_hbm, hub_cols),
+            (own_rows_hbm, own_rows), (own_cols_hbm, own_cols)))
+    ]
+    for copy in small:
+        copy.start()
     tiles_copy = pltpu.make_async_copy(own_hbm, own_v, local_sem.at[0])
     tiles_copy.start()
     hub_copy = pltpu.make_async_copy(hub_hbm.at[b], hub_v.at[b], local_sem.at[1])
@@ -47,24 +61,80 @@
     for h, k in BLK_ORDER:
         pl.semaphore_signal(barrier, inc=1, device_id=(blk_peer(h, k), g), device_id_type=MESH)
 
-    def greet(k, _):
-        pl.semaphore_signal(barrier, inc=1, device_id=(b, lax.rem(g + k, NG)), device_id_type=MESH)
-        return 0
-
-    lax.fori_loop(1, NG, greet, 0)
-
+    for k in (1, 2, 3):
+        pl.semaphore_signal(barrier, inc=1, device_id=(b, quad(k)), device_id_type=MESH)
+    for k in RING:
+        pl.semaphore_signal(barrier, inc=1, device_id=(b, z_peer(k)), device_id_type=MESH)
+
+    for copy in small:
+        copy.wait()
     for d in range(NB):
-        meta[d] = jnp.full((8, T), hub_rows[d, 0] * NB + hub_cols[d, 0], jnp.int32)
+        meta[d] = jnp.full((8, T), hub_rows[d] * NB + hub_cols[d], jnp.int32)
     acc[0] = jnp.zeros((T, T), jnp.float32)
     low = factor[...].astype(jnp.bfloat16)
     gath0[b] = low
 
-    pl.semaphore_wait(barrier, NB - 1 + NG - 1)
+    pl.semaphore_wait(barrier, NB - 1 + 3 + NZ - 1)
+
+    def pass_on(gath, sweep, block, h, k):
+        pltpu.make_async_remote_copy(
+            gath.at[block], gath.at[block], ag_ssem.at[sweep], ag_rsem.at[sweep, block],
+            device_id=(blk_peer(h, k), g), device_id_type=MESH).start()
 
     def send_factor(gath, sweep):
+        for h, k in ((0, 2), (0, 6), (0, 1), (0, 7), (1, 0)):
+            pass_on(gath, sweep, b, h, k)
+
+    def forward_factor(gath, sweep):
+        for k, further in ((6, (2, 1)), (2, (7,)), (7, ()), (1, ()), (5, ()), (3, ()), (4, ())):
+            block = blk_peer(0, k)
+            wait(gath.at[block], ag_rsem.at[sweep, block])
+            for f in further:
+                pass_on(gath, sweep, block, 0, f)
+            pass_on(gath, sweep, block, 1, 0)
+
+    def rest_of_factor(gath, sweep):
+        for k in range(NZ):
+            block = blk_peer(1, k)
+            wait(gath.at[block], ag_rsem.at[sweep, block])
+
+    def gram_start(low, sweep):
+        own, into = ((gram_own0, blk_in0), (gram_own1, blk_in1))[sweep]
+        own[...] = lax.dot_general(
+            low, low, (((0,), (0,)), ((), ())), preferred_element_type=jnp.float32).reshape(NB, 8, T)
         for h, k in BLK_ORDER:
-            pltpu.make_async_remote_copy(
-                gath.at[b], gath.at[b], ag_ssem.at[sweep], ag_rsem.at[sweep],
+            d = blk_peer(h, k)
+            pltpu.make_async_remote_copy(
+                own.at[d], into.at[b], gb_ssem.at[sweep], gb_rsem.at[sweep],
+                device_id=(d, g), device_id_type=MESH).start()
+        into[b] = own[b]
+
+    def gram_quad(sweep):
+        into, nxt = ((blk_in0, quad_in0), (blk_in1, quad_in1))[sweep]
+        wait(into.at[pl.ds(0, NB - 1)], gb_rsem.at[sweep])
+        me = lax.rem(g, 4)
+        nxt[me] = jnp.sum(into[...], axis=0)
+        for k in (2, 1, 3):
+            pltpu.make_async_remote_copy(
+                nxt.at[me], nxt.at[me], gq_ssem.at[sweep], gq_rsem.at[sweep],
+                device_id=(b, quad(k)), device_id_type=MESH).start()
+
+    def gram_z(sweep):
+        into, nxt = ((quad_in0, z_in0), (quad_in1, z_in1))[sweep]
+        wait(into.at[pl.ds(0, 3)], gq_rsem.at[sweep])
+        nxt[z] = jnp.sum(into[...], axis=0)
+        for k in RING:
+            pltpu.make_async_remote_copy(
+                nxt.at[z], nxt.at[z], gz_ssem.at[sweep], gz_rsem.at[sweep],
+                device_id=(b, z_peer(k)), device_id_type=MESH).start()
+
+    def gram_blk(sweep):
+        into, gram = ((z_in0, gram0), (z_in1, gram1))[sweep]
+        wait(into.at[pl.ds(0, NZ - 1)], gz_rsem.at[sweep])
+        gram[b] = jnp.sum(into[...], axis=0)
+        for h, k in BLK_ORDER:
+            pltpu.make_async_remote_copy(
+                gram.at[b], gram.at[b], h_ssem.at[sweep], h_rsem.at[sweep],
                 device_id=(blk_peer(h, k), g), device_id_type=MESH).start()
 
     for h, k in BLK_ORDER:
@@ -72,11 +142,13 @@
         pltpu.make_async_remote_copy(
             meta.at[d], meta_in.at[b], meta_ssem, meta_rsem, device_id=(d, g), device_id_type=MESH).start()
     send_factor(gath0, 0)
+    gram_start(low, 0)
     for h, k in BLK_ORDER:
         d = blk_peer(h, k)
         pltpu.make_async_remote_copy(
             hub_hbm.at[d], hub_v.at[b], hub_ssem, hub_rsem, device_id=(d, g), device_id_type=MESH).start()
     meta_in[b] = meta[b]
+    forward_factor(gath0, 0)
 
     lane = lax.broadcasted_iota(jnp.int32, (8, T), 1)
     sub = lax.broadcasted_iota(jnp.int32, (8, T), 0)
@@ -117,29 +189,18 @@
 
     current = factor[...]
     for sweep in range(ITERS):
-        gath, recv_a, recv_b, recv_c, gram_in, gram = (
-            (gath0, recv_a0, recv_b0, recv_c0, gram_in0, gram0),
-            (gath1, recv_a1, recv_b1, recv_c1, gram_in1, gram1),
+        gath, recv_a, recv_b, recv_c, gram = (
+            (gath0, recv_a0, recv_b0, recv_c0, gram0),
+            (gath1, recv_a1, recv_b1, recv_c1, gram1),
         )[sweep]
         if sweep:
-            gath[b] = current.astype(jnp.bfloat16)
+            low = current.astype(jnp.bfloat16)
+            gath[b] = low
             send_factor(gath, sweep)
-        wait(gath.at[pl.ds(0, NB - 1)], ag_rsem.at[sweep])
-
-        every = gath[...].reshape(NB * T, T)
-        group = lax.dot_general(every, every, (((0,), (0,)), ((), ())), preferred_element_type=jnp.float32)
-        if sweep:
-            wait(gram_in0.at[pl.ds(0, NG - 1)], g_ssem.at[0])
-        gram_own[...] = group.reshape(NB, 8, T)
-
-        def send_gram(k, _):
-            pltpu.make_async_remote_copy(
-                gram_own.at[b], gram_in.at[g], g_ssem.at[sweep], g_rsem.at[sweep],
-                device_id=(b, lax.rem(g + k, NG)), device_id_type=MESH).start()
-            return 0
-
-        lax.fori_loop(1, NG, send_gram, 0)
-        gram_in[g] = gram_own[b]
+            gram_start(low, sweep)
+            forward_factor(gath, sweep)
+        gram_quad(sweep)
+        rest_of_factor(gath, sweep)
 
         if sweep == 0:
             tiles_copy.wait()
@@ -149,14 +210,9 @@
             acc[t + 1] = acc[ptr_s[0, t]] + p
             return 0
 
-        lax.fori_loop(0, OWN, own_step, 0, unroll=8)
-
-        wait(gram_in.at[pl.ds(0, NG - 1)], g_rsem.at[sweep])
-        gram[b] = jnp.sum(gram_in[...], axis=0)
-        for h, k in BLK_ORDER:
-            pltpu.make_async_remote_copy(
-                gram.at[b], gram.at[b], h_ssem.at[sweep], h_rsem.at[sweep],
-                device_id=(blk_peer(h, k), g), device_id_type=MESH).start()
+        lax.fori_loop(0, OWN // 2, own_step, 0, unroll=6)
+        gram_z(sweep)
+        lax.fori_loop(OWN // 2, OWN, own_step, 0, unroll=6)
 
         if sweep == 0:
             hub_copy.wait()
@@ -192,6 +248,7 @@
             pltpu.make_async_remote_copy(
                 send_b.at[zz], recv_b.at[zz], b_ssem, b_rsem.at[sweep, zz],
                 device_id=(b, g + 2 - 4 * xh), device_id_type=MESH).start()
+        gram_blk(sweep)
         wait(recv_a.at[pl.ds(NZ, NZ)], a_rsem.at[sweep, 1])
         total = None
         for k in RING + (0,):
@@ -216,10 +273,12 @@
     out[...] = current
     wait(meta_in.at[pl.ds(0, NB - 1)], meta_ssem)
     wait(hub_v.at[pl.ds(0, NB - 1)], hub_ssem)
-    wait(gram_in1.at[pl.ds(0, NG - 1)], g_ssem.at[1])
     for sweep in range(ITERS):
         wait(gath0.at[pl.ds(0, NB - 1)], ag_ssem.at[sweep])
         wait(gram0.at[pl.ds(0, NB - 1)], h_ssem.at[sweep])
+        wait(gram0.at[pl.ds(0, NB - 1)], gb_ssem.at[sweep])
+        wait(quad_in0.at[pl.ds(0, 3)], gq_ssem.at[sweep])
+        wait(z_in0.at[pl.ds(0, NZ - 1)], gz_ssem.at[sweep])
     wait(send_a, a_ssem)
     wait(send_b, b_ssem)
     wait(send_c.at[pl.ds(0, NZ - 1)], c_ssem)
@@ -228,26 +287,28 @@
 def body(own_tiles, own_rows, own_cols, hub_tiles, hub_rows, hub_cols, factor):
     bf, f32, i32 = jnp.bfloat16, jnp.float32, jnp.int32
     V, S, D = pltpu.VMEM, pltpu.SMEM, pltpu.SemaphoreType.DMA
-    vmem, smem, hbm = (pl.BlockSpec(memory_space=m) for m in (V, S, pl.ANY))
+    vmem, hbm = pl.BlockSpec(memory_space=V), pl.BlockSpec(memory_space=pltpu.HBM)
     return pl.pallas_call(
         kernel,
         out_shape=jax.ShapeDtypeStruct((T, T), f32),
-        in_specs=[hbm, smem, smem, hbm, smem, smem, vmem],
+        in_specs=[hbm] * 7,
         out_specs=vmem,
         scratch_shapes=[
+            S((OWN,), i32), S((OWN,), i32), S((NB,), i32), S((NB,), i32), V((T, T), f32),
             V((OWN, T, T), bf), V((NB, T, T), bf), V((NB, 8, T), i32), V((NB, 8, T), i32),
             V((NB, T, T), bf), V((NB, T, T), bf), V((OWN + NB + 1, T, T), f32), V((8, T), i32), S((8, T), i32),
             V((2 * NZ, T, T), bf), V((NZ, T, T), bf), V((NZ, T, T), bf),
             V((2 * NZ, T, T), bf), V((2 * NZ, T, T), bf), V((NZ, T, T), bf), V((NZ, T, T), bf),
             V((NZ, T, T), bf), V((NZ, T, T), bf),
-            V((NB, 8, T), f32), V((NG, 8, T), f32), V((NG, 8, T), f32), V((NB, 8, T), f32), V((NB, 8, T), f32),
-            D((2,)), D, D, D, D, D,
-            D((2,)), D((2,)), D, D((2, 2)), D, D((2, NZ)), D, D((2,)),
-            D((2,)), D((2,)), D((2,)), D((2,)),
+            V((NB, 8, T), f32), V((NB, 8, T), f32), V((NB, 8, T), f32), V((NB, 8, T), f32), V((4, 8, T), f32), V((4, 8, T), f32),
+            V((NZ, 8, T), f32), V((NZ, 8, T), f32), V((NB, 8, T), f32), V((NB, 8, T), f32),
+            D((7,)), D, D, D, D, D,
+            D((2,)), D((2, NB)), D, D((2, 2)), D, D((2, NZ)), D, D((2,)),
+            D((2,)), D((2,)), D((2,)), D((2,)), D((2,)), D((2,)), D((2,)), D((2,)),
         ],
         compiler_params=pltpu.CompilerParams(
-            collective_id=1, has_side_effects=True, vmem_limit_bytes=48 << 20),
-    )(own_tiles, own_rows, own_cols, hub_tiles.reshape(NB, T, T), hub_rows, hub_cols, factor)
+            collective_id=1, has_side_effects=True, vmem_limit_bytes=63 << 20),
+    )(own_tiles, own_rows, own_cols, hub_tiles.reshape(NB, T, T), hub_rows.reshape(NB), hub_cols.reshape(NB), factor)
 
 
 def solution(mesh):

time: 101 us -> 89.2 us (0.88)
  local copies, waits for them, and re-layouts: 7.4 us -> 1.47 us
  Pallas kernels: 93 us -> 87.6 us
    unnamed x13 -> x1, local copies, waits for them, and re-layouts: 7.4 us -> 1.47 us
    pallas_call x1, Pallas kernels: 93 us -> 87.6 us  [body(): pl.pallas_call(kernel, out_shape=jax.ShapeDtypeStruct((T, T), f32), in_sp...]
where the time goes in v2:
time: 89.2 us; the launch traced here: 89.1 us
  Pallas kernels  87.6 us (98%)
  local copies, waits for them, and re-layouts  1.47 us (2%)
    pallas_call x1, Pallas kernels, body(): pl.pallas_call(kernel, out_shape=jax.ShapeDtypeStruct((T, T), f32), in_sp...  87.6 us

profile of v2, /device:TPU:1, one launch (start us, length us, event | category | flops | bytes accessed | tf_op | source)
XLA Modules:
  0.0 89.1 jit_solution(3298576350574067566)
XLA Ops:
  0.0 87.6 %shard_map.73 = f32[128,128]{1,0:T(8,128)} custom-call(bf16[120,128,128]{2,1,0:T(8,128)(2,1)} %own_hbm.1, s32[120]{0:T(128)} %own_rows_hbm.1, s32[120]{0:T(128)} %own_cols_hbm.1, bf16[16,128,128]{2,1,0:T(8,128)(2,1)} %bitcast.3, s32[16]{0:T(128)} %bitcast.4, s32[16]{0:T(128)} %bitcast.5, f32[128,128]{1,0:T(8,128)} %factor_hbm.1), custom_call_target="tpu_custom_call" | custom-call | tf_op jit(solution)/shard_map/pallas_call | solution.py:291
  87.6 1.5 %copy.9 = f32[128,128]{1,0:T(8,128)} copy(f32[128,128]{1,0:T(8,128)} %shard_map.73) | data formatting | bytes 131072

commit v3 on v2

--- a/solution.py
+++ b/solution.py
@@ -87,6 +87,8 @@
 
     def forward_factor(gath, sweep):
         for k, further in ((6, (2, 1)), (2, (7,)), (7, ()), (1, ()), (5, ()), (3, ()), (4, ())):
+            if k == 5 and sweep == 0:
+                send_hub()
             block = blk_peer(0, k)
             wait(gath.at[block], ag_rsem.at[sweep, block])
             for f in further:
@@ -97,6 +99,12 @@
         for k in range(NZ):
             block = blk_peer(1, k)
             wait(gath.at[block], ag_rsem.at[sweep, block])
+
+    def send_hub():
+        for h, k in BLK_ORDER:
+            d = blk_peer(h, k)
+            pltpu.make_async_remote_copy(
+                hub_hbm.at[d], hub_v.at[b], hub_ssem, hub_rsem, device_id=(d, g), device_id_type=MESH).start()
 
     def gram_start(low, sweep):
         own, into = ((gram_own0, blk_in0), (gram_own1, blk_in1))[sweep]
@@ -143,10 +151,6 @@
             meta.at[d], meta_in.at[b], meta_ssem, meta_rsem, device_id=(d, g), device_id_type=MESH).start()
     send_factor(gath0, 0)
     gram_start(low, 0)
-    for h, k in BLK_ORDER:
-        d = blk_peer(h, k)
-        pltpu.make_async_remote_copy(
-            hub_hbm.at[d], hub_v.at[b], hub_ssem, hub_rsem, device_id=(d, g), device_id_type=MESH).start()
     meta_in[b] = meta[b]
     forward_factor(gath0, 0)
 
@@ -201,6 +205,7 @@
             forward_factor(gath, sweep)
         gram_quad(sweep)
         rest_of_factor(gath, sweep)
+        gram_z(sweep)
 
         if sweep == 0:
             tiles_copy.wait()
@@ -210,9 +215,7 @@
             acc[t + 1] = acc[ptr_s[0, t]] + p
             return 0
 
-        lax.fori_loop(0, OWN // 2, own_step, 0, unroll=6)
-        gram_z(sweep)
-        lax.fori_loop(OWN // 2, OWN, own_step, 0, unroll=6)
+        lax.fori_loop(0, OWN, own_step, 0, unroll=30)
 
         if sweep == 0:
             hub_copy.wait()
@@ -223,7 +226,7 @@
             acc[OWN + t + 1] = acc[ptr_s[1, t]] + p
             return 0
 
-        lax.fori_loop(0, NB, hub_step, 0, unroll=8)
+        lax.fori_loop(0, NB, hub_step, 0, unroll=16)
 
         if sweep:
             wait(send_a, a_ssem)
@@ -241,6 +244,7 @@
             pltpu.make_async_remote_copy(
                 send_a.at[part], recv_a.at[part], a_ssem, a_rsem.at[sweep, j],
                 device_id=(b, g + 1 - 2 * c), device_id_type=MESH).start()
+        gram_blk(sweep)
         wait(recv_a.at[pl.ds(0, NZ)], a_rsem.at[sweep, 0])
         for k in RING + (0,):
             zz = lax.rem(z + k, NZ)
@@ -248,7 +252,6 @@
             pltpu.make_async_remote_copy(
                 send_b.at[zz], recv_b.at[zz], b_ssem, b_rsem.at[sweep, zz],
                 device_id=(b, g + 2 - 4 * xh), device_id_type=MESH).start()
-        gram_blk(sweep)
         wait(recv_a.at[pl.ds(NZ, NZ)], a_rsem.at[sweep, 1])
         total = None
         for k in RING + (0,):

time: 89.2 us -> 79.6 us (0.89)
  Pallas kernels: 87.6 us -> 77.2 us
    pallas_call x1, Pallas kernels: 87.6 us -> 77.2 us  [body(): pl.pallas_call(kernel, out_shape=jax.ShapeDtypeStruct((T, T), f32), in_sp...]
where the time goes in v3:
time: 79.6 us; the launch traced here: 78.7 us
  Pallas kernels  77.2 us (97%)
  local copies, waits for them, and re-layouts  1.47 us (2%)
    pallas_call x1, Pallas kernels, body(): pl.pallas_call(kernel, out_shape=jax.ShapeDtypeStruct((T, T), f32), in_sp...  77.2 us

profile of v3, /device:TPU:1, one launch (start us, length us, event | category | flops | bytes accessed | tf_op | source)
XLA Modules:
  0.0 78.7 jit_solution(11194625170260787324)
XLA Ops:
  0.0 77.2 %shard_map.73 = f32[128,128]{1,0:T(8,128)} custom-call(bf16[120,128,128]{2,1,0:T(8,128)(2,1)} %own_hbm.1, s32[120]{0:T(128)} %own_rows_hbm.1, s32[120]{0:T(128)} %own_cols_hbm.1, bf16[16,128,128]{2,1,0:T(8,128)(2,1)} %bitcast.3, s32[16]{0:T(128)} %bitcast.4, s32[16]{0:T(128)} %bitcast.5, f32[128,128]{1,0:T(8,128)} %factor_hbm.1), custom_call_target="tpu_custom_call" | custom-call | tf_op jit(solution)/shard_map/pallas_call | solution.py:294
  77.2 1.5 %copy.9 = f32[128,128]{1,0:T(8,128)} copy(f32[128,128]{1,0:T(8,128)} %shard_map.73) | data formatting | bytes 131072

commit v4 on v3

--- a/solution.py
+++ b/solution.py
@@ -87,8 +87,10 @@
 
     def forward_factor(gath, sweep):
         for k, further in ((6, (2, 1)), (2, (7,)), (7, ()), (1, ()), (5, ()), (3, ()), (4, ())):
-            if k == 5 and sweep == 0:
+            if k == 1 and sweep == 0:
                 send_hub()
+            if k == 5 and sweep:
+                gram_quad(sweep)
             block = blk_peer(0, k)
             wait(gath.at[block], ag_rsem.at[sweep, block])
             for f in further:
@@ -96,7 +98,9 @@
             pass_on(gath, sweep, block, 1, 0)
 
     def rest_of_factor(gath, sweep):
-        for k in range(NZ):
+        for k in (0, 1, 7, 2, 6, 5, 3, 4):
+            if k == 5:
+                gram_z(sweep)
             block = blk_peer(1, k)
             wait(gath.at[block], ag_rsem.at[sweep, block])
 
@@ -203,9 +207,9 @@
             send_factor(gath, sweep)
             gram_start(low, sweep)
             forward_factor(gath, sweep)
-        gram_quad(sweep)
+        if sweep == 0:
+            gram_quad(sweep)
         rest_of_factor(gath, sweep)
-        gram_z(sweep)
 
         if sweep == 0:
             tiles_copy.wait()
@@ -235,27 +239,25 @@
         for j in range(2):
             hh = lax.rem(xh + 1 + j, 2)
 
-            def lay_a(k, _):
-                send_a[j * NZ + k] = row_sum(k, hh, 1 - c).astype(jnp.bfloat16)
-                return 0
-
-            lax.fori_loop(0, NZ, lay_a, 0, unroll=4)
-            part = pl.ds(j * NZ, NZ)
-            pltpu.make_async_remote_copy(
-                send_a.at[part], recv_a.at[part], a_ssem, a_rsem.at[sweep, j],
-                device_id=(b, g + 1 - 2 * c), device_id_type=MESH).start()
+            for k in RING + (0,):
+                zz = lax.rem(z + k, NZ)
+                at = j * NZ + zz
+                send_a[at] = row_sum(zz, hh, 1 - c).astype(jnp.bfloat16)
+                pltpu.make_async_remote_copy(
+                    send_a.at[at], recv_a.at[at], a_ssem, a_rsem.at[sweep, at],
+                    device_id=(b, g + 1 - 2 * c), device_id_type=MESH).start()
         gram_blk(sweep)
-        wait(recv_a.at[pl.ds(0, NZ)], a_rsem.at[sweep, 0])
         for k in RING + (0,):
             zz = lax.rem(z + k, NZ)
+            wait(recv_a.at[zz], a_rsem.at[sweep, zz])
             send_b[zz] = (row_sum(zz, 1 - xh, c) + recv_a[zz].astype(jnp.float32)).astype(jnp.bfloat16)
             pltpu.make_async_remote_copy(
                 send_b.at[zz], recv_b.at[zz], b_ssem, b_rsem.at[sweep, zz],
                 device_id=(b, g + 2 - 4 * xh), device_id_type=MESH).start()
-        wait(recv_a.at[pl.ds(NZ, NZ)], a_rsem.at[sweep, 1])
         total = None
         for k in RING + (0,):
             zz = lax.rem(z + k, NZ)
+            wait(recv_a.at[NZ + zz], a_rsem.at[sweep, NZ + zz])
             mine = row_sum(zz, xh, c) + recv_a[NZ + zz].astype(jnp.float32)
             wait(recv_b.at[zz], b_rsem.at[sweep, zz])
             total = mine + recv_b[zz].astype(jnp.float32)
@@ -306,7 +308,7 @@
             V((NB, 8, T), f32), V((NB, 8, T), f32), V((NB, 8, T), f32), V((NB, 8, T), f32), V((4, 8, T), f32), V((4, 8, T), f32),
             V((NZ, 8, T), f32), V((NZ, 8, T), f32), V((NB, 8, T), f32), V((NB, 8, T), f32),
             D((7,)), D, D, D, D, D,
-            D((2,)), D((2, NB)), D, D((2, 2)), D, D((2, NZ)), D, D((2,)),
+            D((2,)), D((2, NB)), D, D((2, 2 * NZ)), D, D((2, NZ)), D, D((2,)),
             D((2,)), D((2,)), D((2,)), D((2,)), D((2,)), D((2,)), D((2,)), D((2,)),
         ],
         compiler_params=pltpu.CompilerParams(

time: 79.6 us -> 79.6 us (level)
  Pallas kernels: 77.2 us -> 78 us
where the time goes in v4:
time: 79.6 us; the launch traced here: 79.4 us
  Pallas kernels  78 us (98%)
  local copies, waits for them, and re-layouts  1.47 us (2%)
    pallas_call x1, Pallas kernels, body(): pl.pallas_call(kernel, out_shape=jax.ShapeDtypeStruct((T, T), f32), in_sp...  78 us

profile of v4, /device:TPU:1, one launch (start us, length us, event | category | flops | bytes accessed | tf_op | source)
XLA Modules:
  0.0 79.4 jit_solution(8248191687740933325)
XLA Ops:
  0.0 78.0 %shard_map.73 = f32[128,128]{1,0:T(8,128)} custom-call(bf16[120,128,128]{2,1,0:T(8,128)(2,1)} %own_hbm.1, s32[120]{0:T(128)} %own_rows_hbm.1, s32[120]{0:T(128)} %own_cols_hbm.1, bf16[16,128,128]{2,1,0:T(8,128)(2,1)} %bitcast.3, s32[16]{0:T(128)} %bitcast.4, s32[16]{0:T(128)} %bitcast.5, f32[128,128]{1,0:T(8,128)} %factor_hbm.1), custom_call_target="tpu_custom_call" | custom-call | tf_op jit(solution)/shard_map/pallas_call | solution.py:296
  78.0 1.5 %copy.9 = f32[128,128]{1,0:T(8,128)} copy(f32[128,128]{1,0:T(8,128)} %shard_map.73) | data formatting | bytes 131072

commit v5 on v3

--- a/solution.py
+++ b/solution.py
@@ -96,7 +96,9 @@
             pass_on(gath, sweep, block, 1, 0)
 
     def rest_of_factor(gath, sweep):
-        for k in range(NZ):
+        for k in (0, 1, 7, 2, 6, 5, 3, 4):
+            if k == 5:
+                gram_z(sweep)
             block = blk_peer(1, k)
             wait(gath.at[block], ag_rsem.at[sweep, block])
 
@@ -205,7 +207,6 @@
             forward_factor(gath, sweep)
         gram_quad(sweep)
         rest_of_factor(gath, sweep)
-        gram_z(sweep)
 
         if sweep == 0:
             tiles_copy.wait()
@@ -244,10 +245,11 @@
             pltpu.make_async_remote_copy(
                 send_a.at[part], recv_a.at[part], a_ssem, a_rsem.at[sweep, j],
                 device_id=(b, g + 1 - 2 * c), device_id_type=MESH).start()
-        gram_blk(sweep)
         wait(recv_a.at[pl.ds(0, NZ)], a_rsem.at[sweep, 0])
         for k in RING + (0,):
             zz = lax.rem(z + k, NZ)
+            if k == 6:
+                gram_blk(sweep)
             send_b[zz] = (row_sum(zz, 1 - xh, c) + recv_a[zz].astype(jnp.float32)).astype(jnp.bfloat16)
             pltpu.make_async_remote_copy(
                 send_b.at[zz], recv_b.at[zz], b_ssem, b_rsem.at[sweep, zz],

time: 79.6 us -> 80.4 us (1.010); the launches traced: 78.7 us -> 80.3 us
  Pallas kernels: 77.2 us -> 78.8 us
    pallas_call x1, Pallas kernels: 77.2 us -> 78.8 us  [body(): pl.pallas_call(kernel, out_shape=jax.ShapeDtypeStruct((T, T), f32), in_sp...]
where the time goes in v5:
time: 80.4 us; the launch traced here: 80.3 us
  Pallas kernels  78.8 us (98%)
  local copies, waits for them, and re-layouts  1.47 us (2%)
    pallas_call x1, Pallas kernels, body(): pl.pallas_call(kernel, out_shape=jax.ShapeDtypeStruct((T, T), f32), in_sp...  78.8 us

profile of v5, /device:TPU:1, one launch (start us, length us, event | category | flops | bytes accessed | tf_op | source)
XLA Modules:
  0.0 80.3 jit_solution(7884117294604528320)
XLA Ops:
  0.0 78.8 %shard_map.73 = f32[128,128]{1,0:T(8,128)} custom-call(bf16[120,128,128]{2,1,0:T(8,128)(2,1)} %own_hbm.1, s32[120]{0:T(128)} %own_rows_hbm.1, s32[120]{0:T(128)} %own_cols_hbm.1, bf16[16,128,128]{2,1,0:T(8,128)(2,1)} %bitcast.3, s32[16]{0:T(128)} %bitcast.4, s32[16]{0:T(128)} %bitcast.5, f32[128,128]{1,0:T(8,128)} %factor_hbm.1), custom_call_target="tpu_custom_call" | custom-call | tf_op jit(solution)/shard_map/pallas_call | solution.py:296
  78.8 1.5 %copy.9 = f32[128,128]{1,0:T(8,128)} copy(f32[128,128]{1,0:T(8,128)} %shard_map.73) | data formatting | bytes 131072
